TPU v7x, 128 devices: a whole 4x4x4 slice. The times are simulated.
128 devices in a mesh: dp: 16 (over z, x_hi, core), ctx: 8 (over y, x_lo).
Axes of the slice: x: 4 (x_hi: 2, x_lo: 2; x = x_hi * 2 + x_lo), y: 4, z: 4, core: 2. Of those that a mesh axis runs over, the one named last changes fastest.
Arguments:
- queries: bfloat16 [32768, 2560], P(('dp', 'ctx')), parts along dimension 0, may hold values from -20 to 20
- key_vectors: bfloat16 [32768, 512], P(('dp', 'ctx')), parts along dimension 0, may hold values from -20 to 20
- value_vectors: bfloat16 [32768, 512], P(('dp', 'ctx')), parts along dimension 0, may hold values from -6 to 6
- output_gradient: bfloat16 [32768, 2560], P(('dp', 'ctx')), parts along dimension 0, may hold values from -6 to 6
- tree_mask: int32 [256, 16], P('dp'), parts along dimension 0, may hold values from 0 to 2, as said below
- tile_order: int32 [256], P(('dp', 'ctx')), parts along dimension 0, may hold values from 0 to 15, each once
Outputs:
- query_gradient: bfloat16 [32768, 2560], P(('dp', 'ctx')), parts along dimension 0
- key_gradient: bfloat16 [32768, 512], P(('dp', 'ctx')), parts along dimension 0
- value_gradient: bfloat16 [32768, 512], P(('dp', 'ctx')), parts along dimension 0
There are 16 independent parts, one for each index of `dp`. A program takes and returns all parts, laid end to end along the dimension named above; each array names one. Nothing has to cross between parts.
Inputs may be any that keep to these rules, and one draw needn't show every extreme that they name: `tree_mask`: rows and columns are tiles of 128 tokens in tree order. Entry (i, i) is 2. For j < i the entry is 1 exactly when tile j lies on the path from the root to tile i, where the path of a tile is that of an earlier parent tile plus itself, and tile 1's parent is tile 0. Entries above the diagonal are 0. Stored tile s (rows s * 128 to (s + 1) * 128 - 1 of every token array) holds tree tile tile_order[s]; every tile of the tree appears once.
All inputs are finite; a program needn't handle non-finite values.
Results may differ from a plain program's by a relative error of at most 0.017.
Values may be sent and summed in bfloat16 or wider, within the bound.
No kernel may reach another device: no remote copies, remote signals or barrier semaphores. Data moves between devices by JAX's collectives and lax.ppermute only.
A program may use at most 128 MiB of HBM per device.

v0:
```python
import jax
import jax.numpy as jnp
from jax import lax
from jax.sharding import PartitionSpec as P

QUERY_HEADS = 20
KEY_HEADS = 4
HEAD_WIDTH = 128
QUERIES_PER_KEY = 5


neg_fill = -1e30


def from_behind(x, axis, by):
    devices = lax.axis_size(axis)
    return lax.ppermute(x, axis, [(i, (i + by) % devices) for i in range(devices)])


def tile_codes(query_places, key_places, mask_table, tile_len):
    tile_total = mask_table.shape[0]
    columns = jnp.arange(tile_total, dtype=jnp.int32)
    query_hot = (query_places[:, None] // tile_len == columns[None, :]).astype(jnp.bfloat16)
    key_hot = (key_places[:, None] // tile_len == columns[None, :]).astype(jnp.bfloat16)
    picked = jnp.dot(query_hot, mask_table.astype(jnp.bfloat16), preferred_element_type=jnp.float32)
    code_grid = jnp.dot(picked.astype(jnp.bfloat16), key_hot.T, preferred_element_type=jnp.float32)
    causal = key_places[None, :] <= query_places[:, None]
    return (code_grid == 1.0) | (code_grid == 2.0) & causal


def local(queries, key_vectors, value_vectors, output_gradient, tree_mask, tile_order):
    row_number = queries.shape[0]
    tile_len = row_number // tile_order.shape[0]
    inv_root = HEAD_WIDTH ** (-0.5)
    within = jnp.arange(row_number, dtype=jnp.int32) % tile_len
    query_places = (
        jnp.repeat(tile_order, tile_len, total_repeat_length=row_number) * tile_len + within
    )
    query_head_rows = queries.reshape(row_number, KEY_HEADS, QUERIES_PER_KEY, HEAD_WIDTH)
    gradient_heads = output_gradient.reshape(row_number, KEY_HEADS, QUERIES_PER_KEY, HEAD_WIDTH)
    statistic_shape = (KEY_HEADS, QUERIES_PER_KEY, row_number)

    def pair_scores(key_tile_rows, value_tile_rows):
        key_total = key_tile_rows.shape[0]
        key_head_rows = key_tile_rows.reshape(key_total, KEY_HEADS, HEAD_WIDTH)
        value_head_rows = value_tile_rows.reshape(key_total, KEY_HEADS, HEAD_WIDTH)
        scores = (
            jnp.einsum(
                "tgjd,ugd->gjtu", query_head_rows, key_head_rows, preferred_element_type=jnp.float32
            )
            * inv_root
        )
        prob_grad = jnp.einsum(
            "tgjd,ugd->gjtu", gradient_heads, value_head_rows, preferred_element_type=jnp.float32
        )
        return (scores, prob_grad, key_head_rows)

    def backward_piece(key_tile_rows, value_tile_rows, key_places, log_norm, row_delta):
        key_total = key_tile_rows.shape[0]
        allowed = tile_codes(query_places, key_places, tree_mask, tile_len)

        def backward_compute_pair():
            scores, prob_grad, key_head_rows = pair_scores(key_tile_rows, value_tile_rows)
            weights = jnp.where(allowed, jnp.exp(scores - log_norm[..., None]), 0.0)
            prob_bf = weights.astype(jnp.bfloat16)
            dscore = (weights * (prob_grad - row_delta[..., None])).astype(jnp.bfloat16)
            value_portion = jnp.einsum(
                "gjtu,tgjd->ugd", prob_bf, gradient_heads, preferred_element_type=jnp.float32
            )
            key_portion = jnp.einsum(
                "gjtu,tgjd->ugd", dscore, query_head_rows, preferred_element_type=jnp.float32
            )
            query_part = jnp.einsum(
                "gjtu,ugd->tgjd", dscore, key_head_rows, preferred_element_type=jnp.float32
            )
            return (
                query_part,
                key_portion.reshape(key_total, KEY_HEADS * HEAD_WIDTH),
                value_portion.reshape(key_total, KEY_HEADS * HEAD_WIDTH),
            )

        def backward_skip_pair():
            return (
                jnp.zeros((row_number, KEY_HEADS, QUERIES_PER_KEY, HEAD_WIDTH), jnp.float32),
                jnp.zeros((key_total, KEY_HEADS * HEAD_WIDTH), jnp.float32),
                jnp.zeros((key_total, KEY_HEADS * HEAD_WIDTH), jnp.float32),
            )

        return lax.cond(jnp.any(allowed), backward_compute_pair, backward_skip_pair)

    empty_stats = (
        jnp.full(statistic_shape, neg_fill, jnp.float32),
        jnp.zeros(statistic_shape, jnp.float32),
        jnp.zeros(statistic_shape, jnp.float32),
    )
    query_begin = jnp.zeros((row_number, KEY_HEADS, QUERIES_PER_KEY, HEAD_WIDTH), jnp.float32)
    key_tile_rows = lax.all_gather(key_vectors, "ctx", axis=0, tiled=True)
    value_tile_rows = lax.all_gather(value_vectors, "ctx", axis=0, tiled=True)
    allowed = tile_codes(
        query_places, lax.all_gather(query_places, "ctx", axis=0, tiled=True), tree_mask, tile_len
    )

    def forward_compute_pair():
        row_top, mass_sum, weighted = empty_stats
        scores, prob_grad, key_head_rows = pair_scores(key_tile_rows, value_tile_rows)
        masked = jnp.where(allowed, scores, neg_fill)
        new_top = jnp.maximum(row_top, jnp.max(masked, axis=-1))
        expo_terms = jnp.where(allowed, jnp.exp(scores - new_top[..., None]), 0.0)
        shrink = jnp.exp(row_top - new_top)
        return (
            new_top,
            mass_sum * shrink + jnp.sum(expo_terms, axis=-1),
            weighted * shrink + jnp.sum(expo_terms * prob_grad, axis=-1),
        )

    def forward_skip_pair():
        return empty_stats

    stats = lax.cond(jnp.any(allowed), forward_compute_pair, forward_skip_pair)
    row_top, mass_sum, weighted = stats
    log_norm = row_top + jnp.log(mass_sum)
    row_delta = weighted / mass_sum

    def visit_block(key_tile_rows, value_tile_rows, key_places, key_acc, value_acc, query_acc):
        query_add, key_add, value_add = backward_piece(
            key_tile_rows, value_tile_rows, key_places, log_norm, row_delta
        )
        key_acc, value_acc = (
            from_behind((key_acc + key_add).astype(jnp.bfloat16), "ctx", 1).astype(jnp.float32),
            from_behind((value_acc + value_add).astype(jnp.bfloat16), "ctx", 1).astype(jnp.float32),
        )
        return (key_acc, value_acc, query_acc + query_add)

    def cycle_turn(turn_index, cycle_carry):
        key_tile_rows, value_tile_rows, key_places, key_acc, value_acc, query_acc = cycle_carry
        key_acc, value_acc, query_acc = visit_block(
            key_tile_rows, value_tile_rows, key_places, key_acc, value_acc, query_acc
        )
        key_tile_rows, value_tile_rows, key_places = from_behind(
            (key_tile_rows, value_tile_rows, key_places), "ctx", 1
        )
        return (key_tile_rows, value_tile_rows, key_places, key_acc, value_acc, query_acc)

    gradient_begin = jnp.zeros((row_number, KEY_HEADS * HEAD_WIDTH), jnp.float32)
    cycle_carry = lax.fori_loop(
        0,
        lax.axis_size("ctx") - 1,
        cycle_turn,
        (key_vectors, value_vectors, query_places, gradient_begin, gradient_begin, query_begin),
    )
    key_tile_rows, value_tile_rows, key_places, key_acc, value_acc, query_acc = cycle_carry
    key_acc, value_acc, query_acc = visit_block(
        key_tile_rows, value_tile_rows, key_places, key_acc, value_acc, query_acc
    )
    query_gradient = (
        (query_acc * inv_root).reshape(row_number, QUERY_HEADS * HEAD_WIDTH).astype(jnp.bfloat16)
    )
    key_gradient = (key_acc * inv_root).astype(jnp.bfloat16)
    value_gradient = value_acc.astype(jnp.bfloat16)
    return (query_gradient, key_gradient, value_gradient)


def solution(mesh):
    placed = (
        P(("dp", "ctx"), None),
        P(("dp", "ctx"), None),
        P(("dp", "ctx"), None),
        P(("dp", "ctx"), None),
        P("dp", None),
        P(("dp", "ctx")),
    )
    return jax.shard_map(
        local,
        mesh=mesh,
        in_specs=placed,
        out_specs=(P(("dp", "ctx"), None), P(("dp", "ctx"), None), P(("dp", "ctx"), None)),
        check_vma=False,
    )
```

profile of v0, /device:TPU:0, one launch (start us, length us, event | category | flops | bytes accessed | tf_op | source)
XLA Modules:
  0.0 519.5 jit_solution(12155631289054829569)
XLA Ops:
  16.5 19.1 %all-gather = s32[8,1,256]{2,1,0:T(1,128)S(1)} all-gather(s32[1,1,256]{2,1,0:T(1,128)S(1)} %bitcast.171), channel_id=1, replica_groups=mesh['dp'=16,'ctx'=8] {'ctx'}, dimensions={0}, use_global_device_ids=true | all-gather | bytes 9216 | tf_op jit(solution)/shard_map/all_gather | solution.py:100
  38.3 27.2 %all-gather.4.cloned.1.call-done = bf16[2048,512]{1,0:T(8,128)(2,1)} async-done(((bf16[256,512]{1,0:T(8,128)(2,1)}), bf16[2048,512]{1,0:T(8,128)(2,1)}) %all-gather.4.cloned.1.call-update) | async-done | bytes 2097168 | tf_op jit(solution)/shard_map/all_gather | solution.py:97
  65.5 53.0 %all-gather.6.cloned.1.call-done = bf16[2048,512]{1,0:T(8,128)(2,1)} async-done(((bf16[256,512]{1,0:T(8,128)(2,1)}), bf16[2048,512]{1,0:T(8,128)(2,1)}) %all-gather.6.cloned.1.call-update) | async-done | bytes 2097168 | tf_op jit(solution)/shard_map/all_gather | solution.py:98
  118.5 64.7 %conditional.3 = (f32[4,5,256]{2,1,0:T(8,128)}, f32[4,5,256]{2,1,0:T(8,128)S(1)}, f32[4,5,256]{2,1,0:T(8,128)S(1)}) conditional(s32[]{:T(128)} %convert_element_type.116, () %tuple.70, (pred[256,2048]{1,0:T(8,128)(4,1)S(1)}, bf16[2048,512]{1,0:T(8,128)(2,1)}, bf16[256,4,5,128]{0,3,2,1:T(8,128)(2,1)S(1)}, bf16[2048,512]{1,0:T(8,128)(2,1)}, ...), branch_computations={%region_1.2_spmd, %region_2.6_spmd} | conditional | flops 5494558720 | bytes 143900704 | solution.py:119
  119.5 4.0 reshape.349
  123.5 18.5 %fusion.3 = (f32[4,5,256]{2,1,0:T(8,128)S(1)}, f32[4,2048,256,5]{2,1,3,0:T(8,128)}) fusion(pred[256,2048]{0,1:T(8,128)(4,1)S(1)} %copy.89, bf16[256,4,5,128]{0,3,2,1:T(8,128)(2,1)S(1)} %get-tuple-element.553, bf16[2048,4,128,1]{2,1,0,3:T(4,128)(2,1)} %bitcast.157), kind=kOutput, calls=%fused_computation.5 | convolution fusion | flops 2715806720 | bytes 45895680 | tf_op jit(solution)/shard_map/cond/branch_1_fun/tgjd,ugd->gjtu/dot_general | solution.py:48
  142.6 17.8 %fusion.6 = f32[4,5,256]{2,1,0:T(8,128)S(1)} fusion(f32[4,2048,256,5]{2,1,3,0:T(8,128)} %get-tuple-element.602, f32[4,5,256]{2,1,0:T(8,128)} %broadcast_maximum_fusion, pred[256,2048]{0,1:T(8,128)(4,1)S(1)} %copy.89), kind=kLoop, calls=%fused_computation.8 | loop fusion | flops 41937920 | bytes 42508288 | tf_op jit(solution)/shard_map/cond/branch_1_fun/reduce_sum | solution.py:112
  160.5 4.0 reshape.350
  164.4 18.6 %fusion.2 = f32[4,5,256]{2,1,0:T(8,128)S(1)} fusion(f32[4,2048,256,5]{2,1,3,0:T(8,128)} %get-tuple-element.602, f32[4,5,256]{2,1,0:T(8,128)} %broadcast_maximum_fusion, pred[256,2048]{0,1:T(8,128)(4,1)S(1)} %copy.89, bf16[256,4,5,128]{0,3,2,1:T(8,128)(2,1)} %get-tuple-element.555, bf16[2048,4,128,1]{2,1,0,3:T(4,128)(2,1)} %bitcast.163), kind=kOutput, calls=%fused_computation.2 | convolution fusion | flops 2736778240 | bytes 45916160 | tf_op jit(solution)/shard_map/cond/branch_1_fun/tgjd,ugd->gjtu/dot_general | solution.py:53
  184.0 288.2 %while.28 = (s32[]{:T(128)}, bf16[256,512]{1,0:T(8,128)(2,1)S(1)}, bf16[256,512]{1,0:T(8,128)(2,1)}, s32[256]{0:T(256)S(1)}, f32[256,512]{0,1:T(8,128)}, /*index...) while((s32[]{:T(128)}, bf16[256,512]{1,0:T(8,128)(2,1)S(1)}, ...), condition=%wide.region_10.11_spmd.clone, body=%wide.region_6.10_spmd.clone.sunk | while | flops 1695692800 | bytes 68180520 | solution.py:145
  192.8 16.8 %conditional.7 = (f32[256,4,5,128]{3,0,2,1:T(8,128)}, f32[256,512]{0,1:T(8,128)S(1)}, f32[256,512]{0,1:T(8,128)}) conditional(s32[]{:T(128)} %convert_element_type.152, () %tuple.115, (pred[256,256]{0,1:T(8,128)(4,1)}, bf16[256,512]{1,0:T(8,128)(2,1)}, bf16[256,4,5,128]{0,3,2,1:T(8,128)(2,1)S(1)}, f32[4,5,256]{2,1,0:T(8,128)S(1)}, ...), branch_computations={%region_8.8_spmd, %region_9.9_spmd} | conditional | flops 1690828800 | bytes 50786432 | solution.py:89
  198.1 4.6 fusion.13
  206.3 3.3 fusion.17
  213.6 3.6 select_add_fusion.4
  217.2 3.9 collective-permute-done.3
  237.4 15.4 %collective-permute-start.3 = (bf16[256,512]{0,1:T(8,128)(2,1)S(1)}, bf16[256,512]{0,1:T(8,128)(2,1)S(1)}, u32[]{:S(2)}, u32[]{:S(2)}) collective-permute-start(bf16[256,512]{0,1:T(8,128)(2,1)S(1)} %fusion.94), channel_id=1, source_target_pairs={{0,1},{1,2},{2,3},{3,4},{4,5},{5,6},{6,7},{7,0},{8,9},{9,10},{10,1... | collective-permute-start | bytes 786440 | tf_op jit(solution)/shard_map/while/body/eval_jaxpr/ppermute | solution.py:17
  256.5 4.4 select_add_fusion.4
  274.4 16.8 %conditional.7 = (f32[256,4,5,128]{3,0,2,1:T(8,128)}, f32[256,512]{0,1:T(8,128)S(1)}, f32[256,512]{0,1:T(8,128)}) conditional(s32[]{:T(128)} %convert_element_type.152, () %tuple.115, (pred[256,256]{0,1:T(8,128)(4,1)}, bf16[256,512]{1,0:T(8,128)(2,1)}, bf16[256,4,5,128]{0,3,2,1:T(8,128)(2,1)S(1)}, f32[4,5,256]{2,1,0:T(8,128)S(1)}, ...), branch_computations={%region_8.8_spmd, %region_9.9_spmd} | conditional | flops 1690828800 | bytes 50786432 | solution.py:89
  279.8 4.6 fusion.13
  288.0 3.3 fusion.17
  293.8 3.8 collective-permute-start.4
  297.6 4.4 select_add_fusion.4
  315.0 16.8 %conditional.7 = (f32[256,4,5,128]{3,0,2,1:T(8,128)}, f32[256,512]{0,1:T(8,128)S(1)}, f32[256,512]{0,1:T(8,128)}) conditional(s32[]{:T(128)} %convert_element_type.152, () %tuple.115, (pred[256,256]{0,1:T(8,128)(4,1)}, bf16[256,512]{1,0:T(8,128)(2,1)}, bf16[256,4,5,128]{0,3,2,1:T(8,128)(2,1)S(1)}, f32[4,5,256]{2,1,0:T(8,128)S(1)}, ...), branch_computations={%region_8.8_spmd, %region_9.9_spmd} | conditional | flops 1690828800 | bytes 50786432 | solution.py:89
  320.3 4.6 fusion.13
  328.5 3.3 fusion.17
  337.0 4.4 select_add_fusion.4
  354.4 16.8 %conditional.7 = (f32[256,4,5,128]{3,0,2,1:T(8,128)}, f32[256,512]{0,1:T(8,128)S(1)}, f32[256,512]{0,1:T(8,128)}) conditional(s32[]{:T(128)} %convert_element_type.152, () %tuple.115, (pred[256,256]{0,1:T(8,128)(4,1)}, bf16[256,512]{1,0:T(8,128)(2,1)}, bf16[256,4,5,128]{0,3,2,1:T(8,128)(2,1)S(1)}, f32[4,5,256]{2,1,0:T(8,128)S(1)}, ...), branch_computations={%region_8.8_spmd, %region_9.9_spmd} | conditional | flops 1690828800 | bytes 50786432 | solution.py:89
  359.8 4.6 fusion.13
  368.0 3.3 fusion.17
  375.4 4.4 select_add_fusion.4
  387.8 5.3 %collective-permute-start.1 = (bf16[256,512]{1,0:T(8,128)(2,1)}, bf16[256,512]{1,0:T(8,128)(2,1)}, u32[]{:S(2)}, u32[]{:S(2)}) collective-permute-start(bf16[256,512]{1,0:T(8,128)(2,1)} %copy.185), channel_id=1, source_target_pairs={{0,1},{1,2},{2,3},{3,4},{4,5},{5,6},{6,7},{7,0},{8,9},{9,10},{10,1... | collective-permute-start | bytes 786440 | tf_op jit(solution)/shard_map/while/body/eval_jaxpr/ppermute | solution.py:17
  396.8 16.8 %conditional.7 = (f32[256,4,5,128]{3,0,2,1:T(8,128)}, f32[256,512]{0,1:T(8,128)S(1)}, f32[256,512]{0,1:T(8,128)}) conditional(s32[]{:T(128)} %convert_element_type.152, () %tuple.115, (pred[256,256]{0,1:T(8,128)(4,1)}, bf16[256,512]{1,0:T(8,128)(2,1)}, bf16[256,4,5,128]{0,3,2,1:T(8,128)(2,1)S(1)}, f32[4,5,256]{2,1,0:T(8,128)S(1)}, ...), branch_computations={%region_8.8_spmd, %region_9.9_spmd} | conditional | flops 1690828800 | bytes 50786432 | solution.py:89
  402.1 4.6 fusion.13
  410.3 3.3 fusion.17
  416.1 3.5 collective-permute-start.4
  419.6 4.4 select_add_fusion.4
  424.9 3.7 collective-permute-done.4
  431.8 3.4 collective-permute-start
  440.5 16.8 %conditional.7 = (f32[256,4,5,128]{3,0,2,1:T(8,128)}, f32[256,512]{0,1:T(8,128)S(1)}, f32[256,512]{0,1:T(8,128)}) conditional(s32[]{:T(128)} %convert_element_type.152, () %tuple.115, (pred[256,256]{0,1:T(8,128)(4,1)}, bf16[256,512]{1,0:T(8,128)(2,1)}, bf16[256,4,5,128]{0,3,2,1:T(8,128)(2,1)S(1)}, f32[4,5,256]{2,1,0:T(8,128)S(1)}, ...), branch_computations={%region_8.8_spmd, %region_9.9_spmd} | conditional | flops 1690828800 | bytes 50786432 | solution.py:89
  445.8 4.6 fusion.13
  454.1 3.3 fusion.17
  459.9 4.4 select_add_fusion.4
  464.3 4.3 collective-permute-done.3
  475.1 24.6 %conditional.4 = (f32[256,4,5,128]{0,3,2,1:T(8,128)}, f32[256,512]{1,0:T(8,128)S(1)}, f32[256,512]{1,0:T(8,128)S(1)}) conditional(s32[]{:T(128)} %convert_element_type.117, () %tuple.73, (pred[256,256]{1,0:T(8,128)(4,1)S(1)}, bf16[256,512]{1,0:T(8,128)(2,1)S(1)}, bf16[256,4,5,128]{0,3,2,1:T(8,128)(2,1)S(1)}, f32[4,5,256]{2,1,0:T(8,128)S(1)}, ...), branch_computations={%region_12.13_spmd, %region_13.14_spmd} | conditional | flops 1690828800 | bytes 54587472 | solution.py:89
  479.7 4.5 fusion.27
  488.4 3.3 copy.141
  495.4 4.1 fusion.31
  500.3 3.2 copy.93
  (301 shorter events, 202.2 us)
Async XLA Ops:
  7.2 58.3 %all-gather.4.cloned.1.call-start = ((), (), s32[]{:S(2)}) async-start(), calls=%async_computation | async-start | bytes 2359296 | tf_op jit(solution)/shard_map/all_gather | solution.py:97
  10.7 107.9 %all-gather.6.cloned.1.call-start = ((), (), s32[]{:S(2)}) async-start(), calls=%async_computation.1 | async-start | bytes 2359296 | tf_op jit(solution)/shard_map/all_gather | solution.py:98
  11.5 24.2 %copy-start.6 = (s32[16,16]{1,0:T(8,128)S(1)}, s32[16,16]{1,0:T(8,128)}, u32[]{:S(2)}) copy-start(s32[16,16]{1,0:T(8,128)} %param.20) | copy-start | bytes 3076
  118.5 65.4 %copy-start.1 = (bf16[256,512]{1,0:T(8,128)(2,1)S(1)}, bf16[256,512]{1,0:T(8,128)(2,1)}, u32[]{:S(2)}) copy-start(bf16[256,512]{1,0:T(8,128)(2,1)} %copy.206) | copy-start | bytes 786436
  184.0 41.5 %collective-permute-start.2 = (s32[256]{0:T(256)S(1)}, s32[256]{0:T(256)S(1)}, u32[]{:S(2)}, u32[]{:S(2)}) collective-permute-start(s32[256]{0:T(256)S(1)} %copy.186), channel_id=1, source_target_pairs={{0,1},{1,2},{2,3},{3,4},{4,5},{5,6},{6,7},{7,0},{8,9},{9,10},{10,1... | collective-permute-start | bytes 3080 | tf_op jit(solution)/shard_map/while/body/eval_jaxpr/ppermute | solution.py:17
  184.8 40.7 %collective-permute-start = (bf16[256,512]{1,0:T(8,128)(2,1)}, bf16[256,512]{1,0:T(8,128)(2,1)S(1)}, u32[]{:S(2)}, u32[]{:S(2)}) collective-permute-start(bf16[256,512]{1,0:T(8,128)(2,1)} %copy.184), channel_id=1, source_target_pairs={{0,1},{1,2},{2,3},{3,4},{4,5},{5,6},{6,7},{7,0},{8,9},{9,10},{10,1... | collective-permute-start | bytes 786440 | tf_op jit(solution)/shard_map/while/body/eval_jaxpr/ppermute | solution.py:17
  187.7 37.9 %collective-permute-start.1 = (bf16[256,512]{1,0:T(8,128)(2,1)}, bf16[256,512]{1,0:T(8,128)(2,1)}, u32[]{:S(2)}, u32[]{:S(2)}) collective-permute-start(bf16[256,512]{1,0:T(8,128)(2,1)} %copy.185), channel_id=1, source_target_pairs={{0,1},{1,2},{2,3},{3,4},{4,5},{5,6},{6,7},{7,0},{8,9},{9,10},{10,1... | collective-permute-start | bytes 786440 | tf_op jit(solution)/shard_map/while/body/eval_jaxpr/ppermute | solution.py:17
  197.0 9.3 %slice-start = ((s8[5242880]{0:T(1024)(128)(4,1)}), s8[1048576]{0:T(1024)(128)(4,1)S(1)}, s32[]{:S(2)}) async-start(s8[5242880]{0:T(1024)(128)(4,1)} %bitcast.152), calls=%async_computation.2 | async-start | bytes 2097152 | tf_op jit(solution)/shard_map/while/body/eval_jaxpr/cond
  209.7 11.4 %collective-permute-start.3 = (bf16[256,512]{0,1:T(8,128)(2,1)S(1)}, bf16[256,512]{0,1:T(8,128)(2,1)S(1)}, u32[]{:S(2)}, u32[]{:S(2)}) collective-permute-start(bf16[256,512]{0,1:T(8,128)(2,1)S(1)} %fusion.94), channel_id=1, source_target_pairs={{0,1},{1,2},{2,3},{3,4},{4,5},{5,6},{6,7},{7,0},{8,9},{9,10},{10,1... | collective-permute-start | bytes 786440 | tf_op jit(solution)/shard_map/while/body/eval_jaxpr/ppermute | solution.py:17
  212.4 12.3 %collective-permute-start.4 = (bf16[256,512]{0,1:T(8,128)(2,1)S(1)}, bf16[256,512]{0,1:T(8,128)(2,1)S(1)}, u32[]{:S(2)}, u32[]{:S(2)}) collective-permute-start(bf16[256,512]{0,1:T(8,128)(2,1)S(1)} %fusion.95), channel_id=1, source_target_pairs={{0,1},{1,2},{2,3},{3,4},{4,5},{5,6},{6,7},{7,0},{8,9},{9,10},{10,1... | collective-permute-start | bytes 786440 | tf_op jit(solution)/shard_map/while/body/eval_jaxpr/ppermute | solution.py:17
  225.6 39.9 %collective-permute-start.2 = (s32[256]{0:T(256)S(1)}, s32[256]{0:T(256)S(1)}, u32[]{:S(2)}, u32[]{:S(2)}) collective-permute-start(s32[256]{0:T(256)S(1)} %copy.186), channel_id=1, source_target_pairs={{0,1},{1,2},{2,3},{3,4},{4,5},{5,6},{6,7},{7,0},{8,9},{9,10},{10,1... | collective-permute-start | bytes 3080 | tf_op jit(solution)/shard_map/while/body/eval_jaxpr/ppermute | solution.py:17
  226.3 39.1 %collective-permute-start = (bf16[256,512]{1,0:T(8,128)(2,1)}, bf16[256,512]{1,0:T(8,128)(2,1)S(1)}, u32[]{:S(2)}, u32[]{:S(2)}) collective-permute-start(bf16[256,512]{1,0:T(8,128)(2,1)} %copy.184), channel_id=1, source_target_pairs={{0,1},{1,2},{2,3},{3,4},{4,5},{5,6},{6,7},{7,0},{8,9},{9,10},{10,1... | collective-permute-start | bytes 786440 | tf_op jit(solution)/shard_map/while/body/eval_jaxpr/ppermute | solution.py:17
  229.5 36.0 %collective-permute-start.1 = (bf16[256,512]{1,0:T(8,128)(2,1)}, bf16[256,512]{1,0:T(8,128)(2,1)}, u32[]{:S(2)}, u32[]{:S(2)}) collective-permute-start(bf16[256,512]{1,0:T(8,128)(2,1)} %copy.185), channel_id=1, source_target_pairs={{0,1},{1,2},{2,3},{3,4},{4,5},{5,6},{6,7},{7,0},{8,9},{9,10},{10,1... | collective-permute-start | bytes 786440 | tf_op jit(solution)/shard_map/while/body/eval_jaxpr/ppermute | solution.py:17
  237.4 24.3 %collective-permute-start.3 = (bf16[256,512]{0,1:T(8,128)(2,1)S(1)}, bf16[256,512]{0,1:T(8,128)(2,1)S(1)}, u32[]{:S(2)}, u32[]{:S(2)}) collective-permute-start(bf16[256,512]{0,1:T(8,128)(2,1)S(1)} %fusion.94), channel_id=1, source_target_pairs={{0,1},{1,2},{2,3},{3,4},{4,5},{5,6},{6,7},{7,0},{8,9},{9,10},{10,1... | collective-permute-start | bytes 786440 | tf_op jit(solution)/shard_map/while/body/eval_jaxpr/ppermute | solution.py:17
  254.1 10.4 %collective-permute-start.4 = (bf16[256,512]{0,1:T(8,128)(2,1)S(1)}, bf16[256,512]{0,1:T(8,128)(2,1)S(1)}, u32[]{:S(2)}, u32[]{:S(2)}) collective-permute-start(bf16[256,512]{0,1:T(8,128)(2,1)S(1)} %fusion.95), channel_id=1, source_target_pairs={{0,1},{1,2},{2,3},{3,4},{4,5},{5,6},{6,7},{7,0},{8,9},{9,10},{10,1... | collective-permute-start | bytes 786440 | tf_op jit(solution)/shard_map/while/body/eval_jaxpr/ppermute | solution.py:17
  265.5 39.8 %collective-permute-start.2 = (s32[256]{0:T(256)S(1)}, s32[256]{0:T(256)S(1)}, u32[]{:S(2)}, u32[]{:S(2)}) collective-permute-start(s32[256]{0:T(256)S(1)} %copy.186), channel_id=1, source_target_pairs={{0,1},{1,2},{2,3},{3,4},{4,5},{5,6},{6,7},{7,0},{8,9},{9,10},{10,1... | collective-permute-start | bytes 3080 | tf_op jit(solution)/shard_map/while/body/eval_jaxpr/ppermute | solution.py:17
  266.3 39.0 %collective-permute-start = (bf16[256,512]{1,0:T(8,128)(2,1)}, bf16[256,512]{1,0:T(8,128)(2,1)S(1)}, u32[]{:S(2)}, u32[]{:S(2)}) collective-permute-start(bf16[256,512]{1,0:T(8,128)(2,1)} %copy.184), channel_id=1, source_target_pairs={{0,1},{1,2},{2,3},{3,4},{4,5},{5,6},{6,7},{7,0},{8,9},{9,10},{10,1... | collective-permute-start | bytes 786440 | tf_op jit(solution)/shard_map/while/body/eval_jaxpr/ppermute | solution.py:17
  269.9 35.3 %collective-permute-start.1 = (bf16[256,512]{1,0:T(8,128)(2,1)}, bf16[256,512]{1,0:T(8,128)(2,1)}, u32[]{:S(2)}, u32[]{:S(2)}) collective-permute-start(bf16[256,512]{1,0:T(8,128)(2,1)} %copy.185), channel_id=1, source_target_pairs={{0,1},{1,2},{2,3},{3,4},{4,5},{5,6},{6,7},{7,0},{8,9},{9,10},{10,1... | collective-permute-start | bytes 786440 | tf_op jit(solution)/shard_map/while/body/eval_jaxpr/ppermute | solution.py:17
  278.6 9.3 %slice-start = ((s8[5242880]{0:T(1024)(128)(4,1)}), s8[1048576]{0:T(1024)(128)(4,1)S(1)}, s32[]{:S(2)}) async-start(s8[5242880]{0:T(1024)(128)(4,1)} %bitcast.152), calls=%async_computation.2 | async-start | bytes 2097152 | tf_op jit(solution)/shard_map/while/body/eval_jaxpr/cond
  292.4 9.6 %collective-permute-start.3 = (bf16[256,512]{0,1:T(8,128)(2,1)S(1)}, bf16[256,512]{0,1:T(8,128)(2,1)S(1)}, u32[]{:S(2)}, u32[]{:S(2)}) collective-permute-start(bf16[256,512]{0,1:T(8,128)(2,1)S(1)} %fusion.94), channel_id=1, source_target_pairs={{0,1},{1,2},{2,3},{3,4},{4,5},{5,6},{6,7},{7,0},{8,9},{9,10},{10,1... | collective-permute-start | bytes 786440 | tf_op jit(solution)/shard_map/while/body/eval_jaxpr/ppermute | solution.py:17
  293.8 10.6 %collective-permute-start.4 = (bf16[256,512]{0,1:T(8,128)(2,1)S(1)}, bf16[256,512]{0,1:T(8,128)(2,1)S(1)}, u32[]{:S(2)}, u32[]{:S(2)}) collective-permute-start(bf16[256,512]{0,1:T(8,128)(2,1)S(1)} %fusion.95), channel_id=1, source_target_pairs={{0,1},{1,2},{2,3},{3,4},{4,5},{5,6},{6,7},{7,0},{8,9},{9,10},{10,1... | collective-permute-start | bytes 786440 | tf_op jit(solution)/shard_map/while/body/eval_jaxpr/ppermute | solution.py:17
  305.3 42.2 %collective-permute-start.2 = (s32[256]{0:T(256)S(1)}, s32[256]{0:T(256)S(1)}, u32[]{:S(2)}, u32[]{:S(2)}) collective-permute-start(s32[256]{0:T(256)S(1)} %copy.186), channel_id=1, source_target_pairs={{0,1},{1,2},{2,3},{3,4},{4,5},{5,6},{6,7},{7,0},{8,9},{9,10},{10,1... | collective-permute-start | bytes 3080 | tf_op jit(solution)/shard_map/while/body/eval_jaxpr/ppermute | solution.py:17
  306.0 41.4 %collective-permute-start = (bf16[256,512]{1,0:T(8,128)(2,1)}, bf16[256,512]{1,0:T(8,128)(2,1)S(1)}, u32[]{:S(2)}, u32[]{:S(2)}) collective-permute-start(bf16[256,512]{1,0:T(8,128)(2,1)} %copy.184), channel_id=1, source_target_pairs={{0,1},{1,2},{2,3},{3,4},{4,5},{5,6},{6,7},{7,0},{8,9},{9,10},{10,1... | collective-permute-start | bytes 786440 | tf_op jit(solution)/shard_map/while/body/eval_jaxpr/ppermute | solution.py:17
  309.6 37.8 %collective-permute-start.1 = (bf16[256,512]{1,0:T(8,128)(2,1)}, bf16[256,512]{1,0:T(8,128)(2,1)}, u32[]{:S(2)}, u32[]{:S(2)}) collective-permute-start(bf16[256,512]{1,0:T(8,128)(2,1)} %copy.185), channel_id=1, source_target_pairs={{0,1},{1,2},{2,3},{3,4},{4,5},{5,6},{6,7},{7,0},{8,9},{9,10},{10,1... | collective-permute-start | bytes 786440 | tf_op jit(solution)/shard_map/while/body/eval_jaxpr/ppermute | solution.py:17
  319.2 9.3 %slice-start = ((s8[5242880]{0:T(1024)(128)(4,1)}), s8[1048576]{0:T(1024)(128)(4,1)S(1)}, s32[]{:S(2)}) async-start(s8[5242880]{0:T(1024)(128)(4,1)} %bitcast.152), calls=%async_computation.2 | async-start | bytes 2097152 | tf_op jit(solution)/shard_map/while/body/eval_jaxpr/cond
  332.9 10.9 %collective-permute-start.3 = (bf16[256,512]{0,1:T(8,128)(2,1)S(1)}, bf16[256,512]{0,1:T(8,128)(2,1)S(1)}, u32[]{:S(2)}, u32[]{:S(2)}) collective-permute-start(bf16[256,512]{0,1:T(8,128)(2,1)S(1)} %fusion.94), channel_id=1, source_target_pairs={{0,1},{1,2},{2,3},{3,4},{4,5},{5,6},{6,7},{7,0},{8,9},{9,10},{10,1... | collective-permute-start | bytes 786440 | tf_op jit(solution)/shard_map/while/body/eval_jaxpr/ppermute | solution.py:17
  336.9 9.7 %collective-permute-start.4 = (bf16[256,512]{0,1:T(8,128)(2,1)S(1)}, bf16[256,512]{0,1:T(8,128)(2,1)S(1)}, u32[]{:S(2)}, u32[]{:S(2)}) collective-permute-start(bf16[256,512]{0,1:T(8,128)(2,1)S(1)} %fusion.95), channel_id=1, source_target_pairs={{0,1},{1,2},{2,3},{3,4},{4,5},{5,6},{6,7},{7,0},{8,9},{9,10},{10,1... | collective-permute-start | bytes 786440 | tf_op jit(solution)/shard_map/while/body/eval_jaxpr/ppermute | solution.py:17
  347.5 37.8 %collective-permute-start.2 = (s32[256]{0:T(256)S(1)}, s32[256]{0:T(256)S(1)}, u32[]{:S(2)}, u32[]{:S(2)}) collective-permute-start(s32[256]{0:T(256)S(1)} %copy.186), channel_id=1, source_target_pairs={{0,1},{1,2},{2,3},{3,4},{4,5},{5,6},{6,7},{7,0},{8,9},{9,10},{10,1... | collective-permute-start | bytes 3080 | tf_op jit(solution)/shard_map/while/body/eval_jaxpr/ppermute | solution.py:17
  348.3 37.0 %collective-permute-start = (bf16[256,512]{1,0:T(8,128)(2,1)}, bf16[256,512]{1,0:T(8,128)(2,1)S(1)}, u32[]{:S(2)}, u32[]{:S(2)}) collective-permute-start(bf16[256,512]{1,0:T(8,128)(2,1)} %copy.184), channel_id=1, source_target_pairs={{0,1},{1,2},{2,3},{3,4},{4,5},{5,6},{6,7},{7,0},{8,9},{9,10},{10,1... | collective-permute-start | bytes 786440 | tf_op jit(solution)/shard_map/while/body/eval_jaxpr/ppermute | solution.py:17
  350.8 34.5 %collective-permute-start.1 = (bf16[256,512]{1,0:T(8,128)(2,1)}, bf16[256,512]{1,0:T(8,128)(2,1)}, u32[]{:S(2)}, u32[]{:S(2)}) collective-permute-start(bf16[256,512]{1,0:T(8,128)(2,1)} %copy.185), channel_id=1, source_target_pairs={{0,1},{1,2},{2,3},{3,4},{4,5},{5,6},{6,7},{7,0},{8,9},{9,10},{10,1... | collective-permute-start | bytes 786440 | tf_op jit(solution)/shard_map/while/body/eval_jaxpr/ppermute | solution.py:17
  358.6 9.3 %slice-start = ((s8[5242880]{0:T(1024)(128)(4,1)}), s8[1048576]{0:T(1024)(128)(4,1)S(1)}, s32[]{:S(2)}) async-start(s8[5242880]{0:T(1024)(128)(4,1)} %bitcast.152), calls=%async_computation.2 | async-start | bytes 2097152 | tf_op jit(solution)/shard_map/while/body/eval_jaxpr/cond
  372.4 9.3 %collective-permute-start.3 = (bf16[256,512]{0,1:T(8,128)(2,1)S(1)}, bf16[256,512]{0,1:T(8,128)(2,1)S(1)}, u32[]{:S(2)}, u32[]{:S(2)}) collective-permute-start(bf16[256,512]{0,1:T(8,128)(2,1)S(1)} %fusion.94), channel_id=1, source_target_pairs={{0,1},{1,2},{2,3},{3,4},{4,5},{5,6},{6,7},{7,0},{8,9},{9,10},{10,1... | collective-permute-start | bytes 786440 | tf_op jit(solution)/shard_map/while/body/eval_jaxpr/ppermute | solution.py:17
  374.7 9.7 %collective-permute-start.4 = (bf16[256,512]{0,1:T(8,128)(2,1)S(1)}, bf16[256,512]{0,1:T(8,128)(2,1)S(1)}, u32[]{:S(2)}, u32[]{:S(2)}) collective-permute-start(bf16[256,512]{0,1:T(8,128)(2,1)S(1)} %fusion.95), channel_id=1, source_target_pairs={{0,1},{1,2},{2,3},{3,4},{4,5},{5,6},{6,7},{7,0},{8,9},{9,10},{10,1... | collective-permute-start | bytes 786440 | tf_op jit(solution)/shard_map/while/body/eval_jaxpr/ppermute | solution.py:17
  385.3 44.1 %collective-permute-start.2 = (s32[256]{0:T(256)S(1)}, s32[256]{0:T(256)S(1)}, u32[]{:S(2)}, u32[]{:S(2)}) collective-permute-start(s32[256]{0:T(256)S(1)} %copy.186), channel_id=1, source_target_pairs={{0,1},{1,2},{2,3},{3,4},{4,5},{5,6},{6,7},{7,0},{8,9},{9,10},{10,1... | collective-permute-start | bytes 3080 | tf_op jit(solution)/shard_map/while/body/eval_jaxpr/ppermute | solution.py:17
  386.1 43.3 %collective-permute-start = (bf16[256,512]{1,0:T(8,128)(2,1)}, bf16[256,512]{1,0:T(8,128)(2,1)S(1)}, u32[]{:S(2)}, u32[]{:S(2)}) collective-permute-start(bf16[256,512]{1,0:T(8,128)(2,1)} %copy.184), channel_id=1, source_target_pairs={{0,1},{1,2},{2,3},{3,4},{4,5},{5,6},{6,7},{7,0},{8,9},{9,10},{10,1... | collective-permute-start | bytes 786440 | tf_op jit(solution)/shard_map/while/body/eval_jaxpr/ppermute | solution.py:17
  387.8 41.6 %collective-permute-start.1 = (bf16[256,512]{1,0:T(8,128)(2,1)}, bf16[256,512]{1,0:T(8,128)(2,1)}, u32[]{:S(2)}, u32[]{:S(2)}) collective-permute-start(bf16[256,512]{1,0:T(8,128)(2,1)} %copy.185), channel_id=1, source_target_pairs={{0,1},{1,2},{2,3},{3,4},{4,5},{5,6},{6,7},{7,0},{8,9},{9,10},{10,1... | collective-permute-start | bytes 786440 | tf_op jit(solution)/shard_map/while/body/eval_jaxpr/ppermute | solution.py:17
  401.0 9.3 %slice-start = ((s8[5242880]{0:T(1024)(128)(4,1)}), s8[1048576]{0:T(1024)(128)(4,1)S(1)}, s32[]{:S(2)}) async-start(s8[5242880]{0:T(1024)(128)(4,1)} %bitcast.152), calls=%async_computation.2 | async-start | bytes 2097152 | tf_op jit(solution)/shard_map/while/body/eval_jaxpr/cond
  414.7 9.3 %collective-permute-start.3 = (bf16[256,512]{0,1:T(8,128)(2,1)S(1)}, bf16[256,512]{0,1:T(8,128)(2,1)S(1)}, u32[]{:S(2)}, u32[]{:S(2)}) collective-permute-start(bf16[256,512]{0,1:T(8,128)(2,1)S(1)} %fusion.94), channel_id=1, source_target_pairs={{0,1},{1,2},{2,3},{3,4},{4,5},{5,6},{6,7},{7,0},{8,9},{9,10},{10,1... | collective-permute-start | bytes 786440 | tf_op jit(solution)/shard_map/while/body/eval_jaxpr/ppermute | solution.py:17
  416.1 12.5 %collective-permute-start.4 = (bf16[256,512]{0,1:T(8,128)(2,1)S(1)}, bf16[256,512]{0,1:T(8,128)(2,1)S(1)}, u32[]{:S(2)}, u32[]{:S(2)}) collective-permute-start(bf16[256,512]{0,1:T(8,128)(2,1)S(1)} %fusion.95), channel_id=1, source_target_pairs={{0,1},{1,2},{2,3},{3,4},{4,5},{5,6},{6,7},{7,0},{8,9},{9,10},{10,1... | collective-permute-start | bytes 786440 | tf_op jit(solution)/shard_map/while/body/eval_jaxpr/ppermute | solution.py:17
  429.4 42.8 %collective-permute-start.2 = (s32[256]{0:T(256)S(1)}, s32[256]{0:T(256)S(1)}, u32[]{:S(2)}, u32[]{:S(2)}) collective-permute-start(s32[256]{0:T(256)S(1)} %copy.186), channel_id=1, source_target_pairs={{0,1},{1,2},{2,3},{3,4},{4,5},{5,6},{6,7},{7,0},{8,9},{9,10},{10,1... | collective-permute-start | bytes 3080 | tf_op jit(solution)/shard_map/while/body/eval_jaxpr/ppermute | solution.py:17
  431.8 40.4 %collective-permute-start = (bf16[256,512]{1,0:T(8,128)(2,1)}, bf16[256,512]{1,0:T(8,128)(2,1)S(1)}, u32[]{:S(2)}, u32[]{:S(2)}) collective-permute-start(bf16[256,512]{1,0:T(8,128)(2,1)} %copy.184), channel_id=1, source_target_pairs={{0,1},{1,2},{2,3},{3,4},{4,5},{5,6},{6,7},{7,0},{8,9},{9,10},{10,1... | collective-permute-start | bytes 786440 | tf_op jit(solution)/shard_map/while/body/eval_jaxpr/ppermute | solution.py:17
  436.8 35.4 %collective-permute-start.1 = (bf16[256,512]{1,0:T(8,128)(2,1)}, bf16[256,512]{1,0:T(8,128)(2,1)}, u32[]{:S(2)}, u32[]{:S(2)}) collective-permute-start(bf16[256,512]{1,0:T(8,128)(2,1)} %copy.185), channel_id=1, source_target_pairs={{0,1},{1,2},{2,3},{3,4},{4,5},{5,6},{6,7},{7,0},{8,9},{9,10},{10,1... | collective-permute-start | bytes 786440 | tf_op jit(solution)/shard_map/while/body/eval_jaxpr/ppermute | solution.py:17
  444.7 9.3 %slice-start = ((s8[5242880]{0:T(1024)(128)(4,1)}), s8[1048576]{0:T(1024)(128)(4,1)S(1)}, s32[]{:S(2)}) async-start(s8[5242880]{0:T(1024)(128)(4,1)} %bitcast.152), calls=%async_computation.2 | async-start | bytes 2097152 | tf_op jit(solution)/shard_map/while/body/eval_jaxpr/cond
  458.5 10.1 %collective-permute-start.3 = (bf16[256,512]{0,1:T(8,128)(2,1)S(1)}, bf16[256,512]{0,1:T(8,128)(2,1)S(1)}, u32[]{:S(2)}, u32[]{:S(2)}) collective-permute-start(bf16[256,512]{0,1:T(8,128)(2,1)S(1)} %fusion.94), channel_id=1, source_target_pairs={{0,1},{1,2},{2,3},{3,4},{4,5},{5,6},{6,7},{7,0},{8,9},{9,10},{10,1... | collective-permute-start | bytes 786440 | tf_op jit(solution)/shard_map/while/body/eval_jaxpr/ppermute | solution.py:17
  459.8 11.5 %collective-permute-start.4 = (bf16[256,512]{0,1:T(8,128)(2,1)S(1)}, bf16[256,512]{0,1:T(8,128)(2,1)S(1)}, u32[]{:S(2)}, u32[]{:S(2)}) collective-permute-start(bf16[256,512]{0,1:T(8,128)(2,1)S(1)} %fusion.95), channel_id=1, source_target_pairs={{0,1},{1,2},{2,3},{3,4},{4,5},{5,6},{6,7},{7,0},{8,9},{9,10},{10,1... | collective-permute-start | bytes 786440 | tf_op jit(solution)/shard_map/while/body/eval_jaxpr/ppermute | solution.py:17
  475.1 24.8 %copy-start = (f32[256,512]{0,1:T(8,128)S(1)}, f32[256,512]{0,1:T(8,128)}, u32[]{:S(2)}) copy-start(f32[256,512]{0,1:T(8,128)} %get-tuple-element.468) | copy-start | bytes 1572868
  499.8 8.6 %collective-permute-start.6 = (bf16[256,512]{1,0:T(8,128)(2,1)S(1)}, bf16[256,512]{1,0:T(8,128)(2,1)S(1)}, u32[]{:S(2)}, u32[]{:S(2)}) collective-permute-start(bf16[256,512]{1,0:T(8,128)(2,1)S(1)} %add_convert_fusion), channel_id=1, source_target_pairs={{0,1},{1,2},{2,3},{3,4},{4,5},{5,6},{6,7},{7,0},{8,9},{9,10},{10,1... | collective-permute-start | bytes 786440 | tf_op jit(solution)/shard_map/ppermute | solution.py:17
  500.2 11.0 %collective-permute-start.5 = (bf16[256,512]{1,0:T(8,128)(2,1)S(1)}, bf16[256,512]{1,0:T(8,128)(2,1)S(1)}, u32[]{:S(2)}, u32[]{:S(2)}) collective-permute-start(bf16[256,512]{1,0:T(8,128)(2,1)S(1)} %add_convert_fusion.1), channel_id=1, source_target_pairs={{0,1},{1,2},{2,3},{3,4},{4,5},{5,6},{6,7},{7,0},{8,9},{9,10},{10,1... | collective-permute-start | bytes 786440 | tf_op jit(solution)/shard_map/ppermute | solution.py:17
  (22 other events, 95.6 us)
Sparse Core Ops, SparseCore 0:
  10.8 54.6 all-gather.3
  67.1 51.3 all-gather.5
where the time goes:
time: 521 us; the launch traced here: 519 us
  matrix products  156 us (30%)
  waiting for transfers between devices  113 us (22%)
  other arithmetic  91.1 us (17%)
  local copies, waits for them, and re-layouts  62.3 us (12%)
  starting transfers between devices  55.8 us (11%)
  blocking collectives  19.1 us (4%)
  between operations  15.5 us (3%)
  loops' own time  6.45 us (1%)
    ppermute x37, starting transfers between devices, from_behind(): lax.ppermute(x, axis, [(i, (i + by) % devices) for i in range(devices)])  55.7 us
    all_gather x1, waiting for transfers between devices, local(): value_tile_rows = lax.all_gather(value_vectors, 'ctx', axis=0, tiled=True)  53 us
    dot_general x8, matrix products, pair_scores(): jnp.einsum('tgjd,ugd->gjtu', gradient_heads, value_head_rows, preferred_e...  50.7 us
    dot_general x8, matrix products, pair_scores(): jnp.einsum('tgjd,ugd->gjtu', query_head_rows, key_head_rows, preferred_el...  40.6 us
    ppermute x37, waiting for transfers between devices, from_behind(): lax.ppermute(x, axis, [(i, (i + by) % devices) for i in range(devices)])  32.3 us
    add x7, other arithmetic, visit_block(): return (key_acc, value_acc, query_acc + query_add)  29.9 us
    all_gather x1, waiting for transfers between devices, local(): key_tile_rows = lax.all_gather(key_vectors, 'ctx', axis=0, tiled=True)  27.2 us
    dot_general x7, matrix products, backward_compute_pair(): jnp.einsum('gjtu,tgjd->ugd', prob_bf, gradient_heads, preferred_element_t...  23.8 us
  transfers between devices with their start and end apart: 39, of which 16 were waited for; matrix products, arithmetic and copies ran while one was open for 41% of the time, Pallas kernels for 0%

commit v1 on v0

v1 whole, which is shorter than its diff:
```python
import functools

import jax
import jax.numpy as jnp
from jax import lax
from jax.experimental import pallas as pl
from jax.experimental.pallas import tpu as pltpu
from jax.sharding import PartitionSpec as P

QUERY_HEADS = 20
KEY_HEADS = 4
HEAD_WIDTH = 128
TILE = 128
GROUP = 5
LOG2E = 1.4426950408889634
INV_ROOT = HEAD_WIDTH**-0.5
NEG = -1e30
ROWS = 256
KEY_BLOCKS = 4
KEY_TILES = 16
QUERY_TILES = 4
WIDE = GROUP * TILE
NT_DIMS = (((1,), (1,)), ((), ()))
TN_DIMS = (((0,), (0,)), ((), ()))


def dot(a, b):
    return jnp.dot(a, b, preferred_element_type=jnp.float32)


def kernel(
    ids_ref,
    mask_ref,
    q_own,
    g_own,
    qg_partner,
    kv0,
    kv1,
    kv2,
    kv3,
    dq_own,
    dq_partner,
    out0,
    out1,
    out2,
    out3,
    q_all,
    g_all,
    e_all,
    dp_all,
    top_all,
    dq_acc,
    dk_acc,
    dv_acc,
    k_all,
    v_all,
    list_ref,
):
    blocks = (kv0, kv1, kv2, kv3)
    half = 2 * ROWS
    for b in range(KEY_BLOCKS):
        k_all[b * half : (b + 1) * half, :] = blocks[b][0:half, :]
        v_all[b * half : (b + 1) * half, :] = blocks[b][half : 2 * half, :]
    for t in range(QUERY_TILES):
        for j in range(GROUP):
            to = slice(j * TILE, (j + 1) * TILE)
            if t < 2:
                rows = slice(t * TILE, (t + 1) * TILE)
                q_all[t, to, :] = q_own[rows, to]
                g_all[t, to, :] = g_own[rows, to]
            else:
                rows = slice((t - 2) * TILE, (t - 1) * TILE)
                q_all[t, to, :] = qg_partner[rows, to]
                g_all[t, to, :] = qg_partner[slice(ROWS + (t - 2) * TILE, ROWS + (t - 1) * TILE), to]
    dk_acc[...] = jnp.zeros_like(dk_acc)
    dv_acc[...] = jnp.zeros_like(dv_acc)
    key_row = lax.broadcasted_iota(jnp.int32, (TILE, TILE), 0)
    query_col = lax.broadcasted_iota(jnp.int32, (TILE, TILE), 1)
    causal = key_row <= query_col

    def per_query_tile(t, _):
        my_tile = ids_ref[t]

        def collect(u, count):
            code = mask_ref[my_tile, ids_ref[u]]
            list_ref[count] = u
            return count + jnp.where(code == 1, 1, 0)

        list_ref[0] = t
        odd_end = lax.fori_loop(0, KEY_TILES, collect, 2) - 2
        total = odd_end + 1
        paired = total % 2 == 0
        last = list_ref[odd_end + 1]
        list_ref[1] = jnp.where(paired, last, t)
        rest = jnp.where(paired, odd_end - 1, odd_end)
        chunks = 1 + rest // 2
        q = q_all[t]
        g = g_all[t]

        def tiles_of(c):
            first = pl.multiple_of(list_ref[2 * c] * TILE, TILE)
            second = pl.multiple_of(list_ref[2 * c + 1] * TILE, TILE)
            return first, second

        def rows_of(ref, first, second):
            return jnp.concatenate([ref[pl.ds(first, TILE), :], ref[pl.ds(second, TILE), :]], axis=0)

        def products(c):
            first, second = tiles_of(c)
            k = rows_of(k_all, first, second)
            v = rows_of(v_all, first, second)
            s = lax.dot_general(k, q, NT_DIMS, preferred_element_type=jnp.float32)
            dp = lax.dot_general(v, g, NT_DIMS, preferred_element_type=jnp.float32)
            return s * (INV_ROOT * LOG2E), dp

        s, dp = products(0)
        ok = jnp.concatenate([causal, jnp.broadcast_to(paired, (TILE, TILE))], axis=0)
        s = jnp.where(jnp.concatenate([ok] * GROUP, axis=1), s, NEG)
        top = jnp.max(s, axis=0, keepdims=True)
        e = jnp.exp2(s - top)
        e_all[0] = e
        dp_all[0] = dp
        top_all[0, 0:1, :] = top
        mass = jnp.sum(e, axis=0, keepdims=True)
        weighted = jnp.sum(e * dp, axis=0, keepdims=True)

        def forward(c, carry):
            top, mass, weighted = carry
            s, dp = products(c)
            new_top = jnp.maximum(top, jnp.max(s, axis=0, keepdims=True))
            e = jnp.exp2(s - new_top)
            e_all[c] = e
            dp_all[c] = dp
            top_all[c, 0:1, :] = new_top
            shrink = jnp.exp2(top - new_top)
            return (
                new_top,
                mass * shrink + jnp.sum(e, axis=0, keepdims=True),
                weighted * shrink + jnp.sum(e * dp, axis=0, keepdims=True),
            )

        top, mass, weighted = lax.fori_loop(1, chunks, forward, (top, mass, weighted))
        inv_mass = 1.0 / mass
        delta = weighted * inv_mass
        dq_acc[...] = jnp.zeros_like(dq_acc)

        def backward(c, _):
            first, second = tiles_of(c)
            factor = jnp.exp2(top_all[c, 0:1, :] - top) * inv_mass
            p = e_all[c] * factor
            ds = p * (dp_all[c] - delta)
            p = p.astype(jnp.bfloat16)
            ds = ds.astype(jnp.bfloat16)
            dv = dot(p, g)
            dk = dot(ds, q)
            k = rows_of(k_all, first, second)
            dq_acc[...] += lax.dot_general(ds, k, TN_DIMS, preferred_element_type=jnp.float32)
            dv_acc[pl.ds(first, TILE), :] += dv[:TILE]
            dk_acc[pl.ds(first, TILE), :] += dk[:TILE]
            dv_acc[pl.ds(second, TILE), :] += dv[TILE:]
            dk_acc[pl.ds(second, TILE), :] += dk[TILE:]
            return 0

        lax.fori_loop(0, chunks, backward, 0)
        dq = (dq_acc[...] * INV_ROOT).astype(jnp.bfloat16)

        @pl.when(t < 2)
        def _():
            rows = pl.ds(pl.multiple_of(t * TILE, TILE), TILE)
            for j in range(GROUP):
                to = slice(j * TILE, (j + 1) * TILE)
                dq_own[rows, to] = dq[to, :]

        @pl.when(t >= 2)
        def _():
            rows = pl.ds(pl.multiple_of((t - 2) * TILE, TILE), TILE)
            for j in range(GROUP):
                to = slice(j * TILE, (j + 1) * TILE)
                dq_partner[rows, to] = dq[to, :]

        return 0

    lax.fori_loop(0, QUERY_TILES, per_query_tile, 0)
    for b, out in enumerate((out0, out1, out2, out3)):
        rows = slice(b * half, (b + 1) * half)
        out[0:half, :] = dk_acc[rows, :].astype(out.dtype)
        out[half : 2 * half, :] = dv_acc[rows, :].astype(out.dtype)


def head_backward(ids, mask, q_own, g_own, qg_partner, blocks):
    vmem = pl.BlockSpec(memory_space=pltpu.VMEM)
    smem = pl.BlockSpec(memory_space=pltpu.SMEM)
    flops = 8 * 10 * 2 * QUERY_TILES * TILE * TILE * WIDE
    return pl.pallas_call(
        kernel,
        out_shape=(
            jax.ShapeDtypeStruct((ROWS, WIDE), jnp.bfloat16),
            jax.ShapeDtypeStruct((ROWS, WIDE), jnp.bfloat16),
            jax.ShapeDtypeStruct((4 * ROWS, HEAD_WIDTH), jnp.float32),
            jax.ShapeDtypeStruct((4 * ROWS, HEAD_WIDTH), jnp.bfloat16),
            jax.ShapeDtypeStruct((4 * ROWS, HEAD_WIDTH), jnp.bfloat16),
            jax.ShapeDtypeStruct((4 * ROWS, HEAD_WIDTH), jnp.bfloat16),
        ),
        in_specs=[smem, smem] + [vmem] * 7,
        out_specs=(vmem,) * 6,
        scratch_shapes=[
            pltpu.VMEM((QUERY_TILES, WIDE, HEAD_WIDTH), jnp.bfloat16),
            pltpu.VMEM((QUERY_TILES, WIDE, HEAD_WIDTH), jnp.bfloat16),
            pltpu.VMEM((KEY_TILES // 2, 2 * TILE, WIDE), jnp.float32),
            pltpu.VMEM((KEY_TILES // 2, 2 * TILE, WIDE), jnp.float32),
            pltpu.VMEM((KEY_TILES // 2, 8, WIDE), jnp.float32),
            pltpu.VMEM((WIDE, HEAD_WIDTH), jnp.float32),
            pltpu.VMEM((KEY_TILES * TILE, HEAD_WIDTH), jnp.float32),
            pltpu.VMEM((KEY_TILES * TILE, HEAD_WIDTH), jnp.float32),
            pltpu.VMEM((KEY_TILES * TILE, HEAD_WIDTH), jnp.bfloat16),
            pltpu.VMEM((KEY_TILES * TILE, HEAD_WIDTH), jnp.bfloat16),
            pltpu.SMEM((KEY_TILES + 4,), jnp.int32),
        ],
        compiler_params=pltpu.CompilerParams(vmem_limit_bytes=40 * 1024 * 1024),
        cost_estimate=pl.CostEstimate(flops=flops, bytes_accessed=6_000_000, transcendentals=0),
    )(ids, mask, q_own, g_own, qg_partner, *blocks)


def ring_pairs(dy, dx):
    pairs = []
    for c in range(8):
        y, x = divmod(c, 2)
        pairs.append((c, ((y + dy) % 4) * 2 + (x + dx) % 2))
    return pairs


def move(value, dy, dx):
    return lax.ppermute(value, "ctx", ring_pairs(dy, dx))


def local(queries, key_vectors, value_vectors, output_gradient, tree_mask, tile_order):
    x = lax.axis_index("ctx") % 2

    def columns(array, side, head, width):
        return lax.dynamic_slice_in_dim(array, (2 * side + head) * width, width, axis=1)

    ids_row = jnp.pad(tile_order.astype(jnp.bfloat16), (0, HEAD_WIDTH - 2))
    ids_rows = jnp.broadcast_to(ids_row[None, :], (16, HEAD_WIDTH))
    sent = jnp.concatenate(
        [columns(a, 1 - x, h, HEAD_WIDTH) for h in range(2) for a in (key_vectors, value_vectors)]
        + [ids_rows],
        axis=0,
    )
    got = move(sent, 0, 1)
    partner_ids = got[4 * ROWS : 4 * ROWS + 16]
    both_ids = ids_rows + jnp.roll(partner_ids, 2, axis=1)

    partner_qg = [
        move(
            jnp.concatenate(
                [
                    columns(queries, 1 - x, h, WIDE),
                    columns(output_gradient, 1 - x, h, WIDE),
                ],
                axis=0,
            ),
            0,
            1,
        )
        for h in range(2)
    ]
    steps = (1, -1, 2)
    query_own, query_back, home = [], [], []
    ids = None
    for h in range(2):
        mine = jnp.concatenate(
            [
                columns(key_vectors, x, h, HEAD_WIDTH),
                got[2 * h * ROWS : (2 * h + 1) * ROWS],
                columns(value_vectors, x, h, HEAD_WIDTH),
                got[(2 * h + 1) * ROWS : (2 * h + 2) * ROWS],
                both_ids,
            ],
            axis=0,
        )
        arrived = [move(mine, s, 0) for s in steps]
        if ids is None:
            ids = jnp.concatenate([b[4 * ROWS, 0:4] for b in [mine] + arrived]).astype(jnp.int32)
        outs = head_backward(
            ids,
            tree_mask,
            columns(queries, x, h, WIDE),
            columns(output_gradient, x, h, WIDE),
            partner_qg[h],
            [mine] + arrived,
        )
        query_own.append(outs[0])
        query_back.append(move(outs[1], 0, 1))
        total = outs[2]
        for s, part in zip(steps, outs[3:]):
            total = total + move(part, -s, 0).astype(jnp.float32)
        away = jnp.concatenate([total[ROWS : 2 * ROWS], total[3 * ROWS : 4 * ROWS]], axis=0)
        back = move(away.astype(jnp.bfloat16), 0, 1).astype(jnp.float32)
        home.append((total[0:ROWS], total[2 * ROWS : 3 * ROWS], back[0:ROWS], back[ROWS:]))
    first = x == 0

    def arrange(own, other):
        low = [jnp.where(first, a, b) for a, b in zip(own, other)]
        high = [jnp.where(first, b, a) for a, b in zip(own, other)]
        return jnp.concatenate(low + high, axis=1)

    query_gradient = arrange(query_own, query_back)
    key_gradient = arrange([h[0] for h in home], [h[2] for h in home]) * INV_ROOT
    value_gradient = arrange([h[1] for h in home], [h[3] for h in home])
    return query_gradient, key_gradient.astype(jnp.bfloat16), value_gradient.astype(jnp.bfloat16)


def solution(mesh):
    placed = (
        P(("dp", "ctx"), None),
        P(("dp", "ctx"), None),
        P(("dp", "ctx"), None),
        P(("dp", "ctx"), None),
        P("dp", None),
        P(("dp", "ctx")),
    )
    return jax.shard_map(
        local,
        mesh=mesh,
        in_specs=placed,
        out_specs=(P(("dp", "ctx"), None), P(("dp", "ctx"), None), P(("dp", "ctx"), None)),
        check_vma=False,
    )
```

time: 521 us -> 87.3 us (0.17)
  the two profiles are of different devices: /device:TPU:0 before, /device:TPU:43 now
where the time goes in v1:
time: 87.3 us; the launch traced here: 86.5 us
  Pallas kernels  25.5 us (29%)
  waiting for transfers between devices  24.6 us (28%)
  starting transfers between devices  24.1 us (28%)
  other arithmetic  5.82 us (7%)
  local copies, waits for them, and re-layouts  5.63 us (6%)
    pallas_call x2, Pallas kernels, head_backward(): pl.pallas_call(kernel, out_shape=(jax.ShapeDtypeStruct((ROWS, WIDE), jnp....  25.5 us
    ppermute x19, waiting for transfers between devices, move(): return lax.ppermute(value, 'ctx', ring_pairs(dy, dx))  24.6 us
    ppermute x19, starting transfers between devices, move(): return lax.ppermute(value, 'ctx', ring_pairs(dy, dx))  24.1 us
    unnamed x11, local copies, waits for them, and re-layouts  3.59 us
    dynamic_slice x1, local copies, waits for them, and re-layouts, columns(): lax.dynamic_slice_in_dim(array, (2 * side + head) * width, width, axis=1)  1.91 us
    concatenate x2, other arithmetic, arrange(): return jnp.concatenate(low + high, axis=1)  1.89 us
    concatenate x2, other arithmetic, local(): jnp.concatenate([columns(queries, 1 - x, h, WIDE), columns(output_gradien...  1.81 us
  transfers between devices with their start and end apart: 19, of which 9 were waited for; matrix products, arithmetic and copies ran while one was open for 7% of the time, Pallas kernels for 29%

profile of v1, /device:TPU:43, one launch (start us, length us, event | category | flops | bytes accessed | tf_op | source)
XLA Modules:
  0.0 86.5 jit_solution(10267859629193480280)
XLA Ops:
  0.7 0.8 dynamic-slice_dynamic-update-slice_fusion.7
  1.5 0.9 dynamic-slice_dynamic-update-slice_fusion.6
  2.4 0.9 %dynamic-slice_dynamic-update-slice_fusion.1 = (bf16[1040,128]{1,0:T(8,128)(2,1)S(1)}, bf16[1040,128]{1,0:T(8,128)(2,1)S(1)}, bf16[1040,128]{1,0:T(8,128)(2,1)S(1)}) fusion(bf16[256,512]{1,0:T(8,128)(2,1)} %param.7, s32[]{:T(128)S(6)} %select_n.105, bf16[1040,128]{1,0:T(8,128)(2,1)S(1)} %dynamic-slice_dynamic-update-slice_fusion.6, s32[]{:T(128)S(6)} %select_n.98, ...), kind=kLoop, calls=%fused_computation.27 | loop fusion | bytes 393228
  3.3 0.9 dynamic-slice_dynamic-update-slice_fusion.4
  4.2 0.7 convert_element_type.38
  4.9 0.3 collective-permute-start
  5.2 1.9 %constant_dynamic-slice_fusion.4 = (bf16[256,640]{1,0:T(8,128)(2,1)S(1)}, bf16[256,640]{1,0:T(8,128)(2,1)S(1)}, bf16[256,640]{1,0:T(8,128)(2,1)S(1)}, bf16[256,6...) fusion(bf16[256,2560]{1,0:T(8,128)(2,1)} %param.9, ...), kind=kLoop, calls=%fused_computation.42 | loop fusion | bytes 5242896 | tf_op jit(solution)/shard_map/dynamic_slice | solution.py:240
  7.1 0.0 copy-start.1
  7.1 0.9 %pad_maximum_fusion.1 = bf16[512,640]{1,0:T(8,128)(2,1)} fusion(bf16[256,640]{1,0:T(8,128)(2,1)S(1)} %get-tuple-element.37, bf16[256,640]{1,0:T(8,128)(2,1)S(1)} %get-tuple-element.69), kind=kLoop, calls=%fused_computation.1 | loop fusion | flops 1310720 | bytes 1310720 | tf_op jit(solution)/shard_map/concatenate | solution.py:255
  8.0 1.2 %collective-permute-start.4 = (bf16[512,640]{1,0:T(8,128)(2,1)}, bf16[512,640]{1,0:T(8,128)(2,1)S(1)}, u32[]{:S(2)}, u32[]{:S(2)}) collective-permute-start(bf16[512,640]{1,0:T(8,128)(2,1)} %pad_maximum_fusion.1), channel_id=1, source_target_pairs={{0,1},{1,0},{2,3},{3,2},{4,5},{5,4},{6,7},{7,6},{8,9},{9,8},{10,11... | collective-permute-start | bytes 1966088 | tf_op jit(solution)/shard_map/ppermute | solution.py:233
  9.2 2.9 %collective-permute-done = bf16[1040,128]{1,0:T(8,128)(2,1)S(1)} collective-permute-done((bf16[1040,128]{1,0:T(8,128)(2,1)S(1)}, bf16[1040,128]{1,0:T(8,128)(2,1)S(1)}, u32[]{:S(2)}, u32[]{:S(2)}) %collective-permute-start) | collective-permute-done | bytes 266272 | tf_op jit(solution)/shard_map/ppermute | solution.py:233
  12.3 0.1 slice.97
  12.4 0.1 constant_dynamic-update-slice_fusion.2
  12.5 2.0 %collective-permute-start.3 = (bf16[1040,128]{1,0:T(8,128)(2,1)S(1)}, bf16[1040,128]{1,0:T(8,128)(2,1)S(1)}, u32[]{:S(2)}, u32[]{:S(2)}) collective-permute-start(bf16[1040,128]{1,0:T(8,128)(2,1)S(1)} %constant_dynamic-update-slice_fusion.1.kv0), channel_id=1, source_target_pairs={{0,4},{1,5},{2,6},{3,7},{4,0},{5,1},{6,2},{7,3},{8,12},{9,13},{10,... | collective-permute-start | bytes 798728 | tf_op jit(solution)/shard_map/ppermute | solution.py:233
  14.5 0.9 %pad_maximum_fusion.2 = bf16[512,640]{1,0:T(8,128)(2,1)} fusion(bf16[256,640]{1,0:T(8,128)(2,1)S(1)} %get-tuple-element.39, bf16[256,640]{1,0:T(8,128)(2,1)S(1)} %get-tuple-element.67), kind=kLoop, calls=%fused_computation.2 | loop fusion | flops 1310720 | bytes 1310720 | tf_op jit(solution)/shard_map/concatenate | solution.py:255
  15.4 0.3 collective-permute-start.6
  15.6 1.1 %collective-permute-start.2 = (bf16[1040,128]{1,0:T(8,128)(2,1)S(1)}, bf16[1040,128]{1,0:T(8,128)(2,1)S(1)}, u32[]{:S(2)}, u32[]{:S(2)}) collective-permute-start(bf16[1040,128]{1,0:T(8,128)(2,1)S(1)} %constant_dynamic-update-slice_fusion.1.kv0), channel_id=1, source_target_pairs={{0,6},{1,7},{2,0},{3,1},{4,2},{5,3},{6,4},{7,5},{8,14},{9,15},{10,... | collective-permute-start | bytes 798728 | tf_op jit(solution)/shard_map/ppermute | solution.py:233
  16.7 0.4 collective-permute-start.1
  17.1 2.2 %collective-permute-done.3.kv3 = bf16[1040,128]{1,0:T(8,128)(2,1)S(1)} collective-permute-done((bf16[1040,128]{1,0:T(8,128)(2,1)S(1)}, bf16[1040,128]{1,0:T(8,128)(2,1)S(1)}, u32[]{:S(2)}, u32[]{:S(2)}) %collective-permute-start.3) | collective-permute-done | bytes 266272 | tf_op jit(solution)/shard_map/ppermute | solution.py:233
  19.4 1.3 %collective-permute-start.7 = (bf16[1040,128]{1,0:T(8,128)(2,1)S(1)}, bf16[1040,128]{1,0:T(8,128)(2,1)S(1)}, u32[]{:S(2)}, u32[]{:S(2)}) collective-permute-start(bf16[1040,128]{1,0:T(8,128)(2,1)S(1)} %get-tuple-element.31.kv0), channel_id=1, source_target_pairs={{0,2},{1,3},{2,4},{3,5},{4,6},{5,7},{6,0},{7,1},{8,10},{9,11},{10,... | collective-permute-start | bytes 798728 | tf_op jit(solution)/shard_map/ppermute | solution.py:233
  20.7 5.9 %collective-permute-done.2.kv2 = bf16[1040,128]{1,0:T(8,128)(2,1)S(1)} collective-permute-done((bf16[1040,128]{1,0:T(8,128)(2,1)S(1)}, bf16[1040,128]{1,0:T(8,128)(2,1)S(1)}, u32[]{:S(2)}, u32[]{:S(2)}) %collective-permute-start.2) | collective-permute-done | bytes 266272 | tf_op jit(solution)/shard_map/ppermute | solution.py:233
  26.6 0.0 collective-permute-start.8
  26.6 0.0 collective-permute-done.1.kv1
  26.6 2.0 %collective-permute-start.9 = (bf16[1040,128]{1,0:T(8,128)(2,1)S(1)}, bf16[1040,128]{1,0:T(8,128)(2,1)S(1)}, u32[]{:S(2)}, u32[]{:S(2)}) collective-permute-start(bf16[1040,128]{1,0:T(8,128)(2,1)S(1)} %get-tuple-element.31.kv0), channel_id=1, source_target_pairs={{0,4},{1,5},{2,6},{3,7},{4,0},{5,1},{6,2},{7,3},{8,12},{9,13},{10,... | collective-permute-start | bytes 798728 | tf_op jit(solution)/shard_map/ppermute | solution.py:233
  28.6 0.1 maximum_convert_fusion.ids_ref
  28.7 12.7 %shard_map.85 = (bf16[256,640]{1,0:T(8,128)(2,1)S(1)}, bf16[256,640]{1,0:T(8,128)(2,1)S(1)}, f32[1024,128]{1,0:T(8,128)S(1)}, bf16[1024,128]{1,0:T(8,128)(2,1)S(...) custom-call(s32[16]{0:T(128)S(1)} %maximum_convert_fusion.ids_ref, s32[16,16]{1,0:T(8,128)S(1)} %copy-done, ...), custom_call_target="tpu_custom_call" | custom-call | flops 6710886400 | bytes 6000000 | tf_op jit(solution)/shard_map/pallas_call | solution.py:194
  41.5 4.5 %collective-permute-start.11 = (bf16[1024,128]{1,0:T(8,128)(2,1)S(1)}, bf16[1024,128]{1,0:T(8,128)(2,1)S(1)}, u32[]{:S(2)}, u32[]{:S(2)}) collective-permute-start(bf16[1024,128]{1,0:T(8,128)(2,1)S(1)} %get-tuple-element.20), channel_id=1, source_target_pairs={{0,6},{1,7},{2,0},{3,1},{4,2},{5,3},{6,4},{7,5},{8,14},{9,15},{10,... | collective-permute-start | bytes 786440 | tf_op jit(solution)/shard_map/ppermute | solution.py:233
  46.0 0.0 collective-permute-done.7.kv1
  46.0 2.5 %collective-permute-start.13 = (bf16[1024,128]{1,0:T(8,128)(2,1)S(1)}, bf16[1024,128]{1,0:T(8,128)(2,1)S(1)}, u32[]{:S(2)}, u32[]{:S(2)}) collective-permute-start(bf16[1024,128]{1,0:T(8,128)(2,1)S(1)} %get-tuple-element.22), channel_id=1, source_target_pairs={{0,4},{1,5},{2,6},{3,7},{4,0},{5,1},{6,2},{7,3},{8,12},{9,13},{10,... | collective-permute-start | bytes 786440 | tf_op jit(solution)/shard_map/ppermute | solution.py:233
  48.5 12.7 %shard_map.86 = (bf16[256,640]{1,0:T(8,128)(2,1)S(1)}, bf16[256,640]{1,0:T(8,128)(2,1)S(1)}, f32[1024,128]{1,0:T(8,128)S(1)}, bf16[1024,128]{1,0:T(8,128)(2,1)S(...) custom-call(s32[16]{0:T(128)S(1)} %maximum_convert_fusion.ids_ref, s32[16,16]{1,0:T(8,128)S(1)} %copy-done, ...), custom_call_target="tpu_custom_call" | custom-call | flops 6710886400 | bytes 6000000 | tf_op jit(solution)/shard_map/pallas_call | solution.py:194
  61.2 2.8 %collective-permute-start.15 = (bf16[1024,128]{1,0:T(8,128)(2,1)S(1)}, bf16[1024,128]{1,0:T(8,128)(2,1)S(1)}, u32[]{:S(2)}, u32[]{:S(2)}) collective-permute-start(bf16[1024,128]{1,0:T(8,128)(2,1)S(1)} %get-tuple-element.24), channel_id=1, source_target_pairs={{0,6},{1,7},{2,0},{3,1},{4,2},{5,3},{6,4},{7,5},{8,14},{9,15},{10,... | collective-permute-start | bytes 786440 | tf_op jit(solution)/shard_map/ppermute | solution.py:233
  64.0 3.8 %collective-permute-start.17 = (bf16[1024,128]{1,0:T(8,128)(2,1)S(1)}, bf16[1024,128]{1,0:T(8,128)(2,1)S(1)}, u32[]{:S(2)}, u32[]{:S(2)}) collective-permute-start(bf16[1024,128]{1,0:T(8,128)(2,1)S(1)} %get-tuple-element.26), channel_id=1, source_target_pairs={{0,4},{1,5},{2,6},{3,7},{4,0},{5,1},{6,2},{7,3},{8,12},{9,13},{10,... | collective-permute-start | bytes 786440 | tf_op jit(solution)/shard_map/ppermute | solution.py:233
  67.8 1.5 %collective-permute-start.10 = (bf16[256,640]{1,0:T(8,128)(2,1)S(1)}, bf16[256,640]{1,0:T(8,128)(2,1)S(1)}, u32[]{:S(2)}, u32[]{:S(2)}) collective-permute-start(bf16[256,640]{1,0:T(8,128)(2,1)S(1)} %get-tuple-element.18), channel_id=1, source_target_pairs={{0,1},{1,0},{2,3},{3,2},{4,5},{5,4},{6,7},{7,6},{8,9},{9,8},{10,11... | collective-permute-start | bytes 983048 | tf_op jit(solution)/shard_map/ppermute | solution.py:233
  69.3 0.1 fusion.1
  69.5 0.2 collective-permute-start.14
  69.6 0.4 collective-permute-done.16
  70.1 1.6 %collective-permute-done.17 = bf16[1024,128]{1,0:T(8,128)(2,1)S(1)} collective-permute-done((bf16[1024,128]{1,0:T(8,128)(2,1)S(1)}, bf16[1024,128]{1,0:T(8,128)(2,1)S(1)}, u32[]{:S(2)}, u32[]{:S(2)}) %collective-permute-start.17) | collective-permute-done | bytes 262176 | tf_op jit(solution)/shard_map/ppermute | solution.py:233
  71.7 0.1 fusion.2
  71.9 0.3 collective-permute-start.18
  72.2 5.4 %collective-permute-done.5 = bf16[256,640]{1,0:T(8,128)(2,1)S(1)} collective-permute-done((bf16[256,640]{1,0:T(8,128)(2,1)S(1)}, bf16[256,640]{1,0:T(8,128)(2,1)S(1)}, u32[]{:S(2)}, u32[]{:S(2)}) %collective-permute-start.5) | collective-permute-done | bytes 327712 | tf_op jit(solution)/shard_map/ppermute | solution.py:233
  77.6 0.1 broadcast_select_fusion.3
  77.7 4.4 %collective-permute-done.10 = bf16[256,640]{1,0:T(8,128)(2,1)S(1)} collective-permute-done((bf16[256,640]{1,0:T(8,128)(2,1)S(1)}, bf16[256,640]{1,0:T(8,128)(2,1)S(1)}, u32[]{:S(2)}, u32[]{:S(2)}) %collective-permute-start.10) | collective-permute-done | bytes 327712 | tf_op jit(solution)/shard_map/ppermute | solution.py:233
  82.1 0.1 broadcast_select_fusion.2
  82.2 1.2 %pad_maximum_fusion = bf16[256,2560]{1,0:T(8,128)(2,1)} fusion(bf16[256,640]{1,0:T(8,128)(2,1)S(1)} %get-tuple-element.52, bf16[256,640]{1,0:T(8,128)(2,1)S(1)} %get-tuple-element.50, bf16[256,640]{1,0:T(8,128)(2,1)S(1)} %get-tuple-element.51, bf16[256,640]{1,0:T(8,128)(2,1)S(1)} %get-tuple-element.49), kind=kLoop, calls=%fused_computation | loop fusion | flops 5242880 | bytes 2621440 | tf_op jit(solution)/shard_map/concatenate | solution.py:305
  83.4 0.2 collective-permute-done.14
  83.6 1.3 %collective-permute-done.18 = bf16[512,128]{1,0:T(8,128)(2,1)S(1)} collective-permute-done((bf16[512,128]{1,0:T(8,128)(2,1)S(1)}, bf16[512,128]{1,0:T(8,128)(2,1)S(1)}, u32[]{:S(2)}, u32[]{:S(2)}) %collective-permute-start.18) | collective-permute-done | bytes 131104 | tf_op jit(solution)/shard_map/ppermute | solution.py:233
  85.0 0.7 pad_maximum_fusion.3
  85.8 0.7 fusion
  (35 shorter events, 0.3 us)
Async XLA Ops:
  4.9 7.3 %collective-permute-start = (bf16[1040,128]{1,0:T(8,128)(2,1)S(1)}, bf16[1040,128]{1,0:T(8,128)(2,1)S(1)}, u32[]{:S(2)}, u32[]{:S(2)}) collective-permute-start(bf16[1040,128]{1,0:T(8,128)(2,1)S(1)} %constant_dynamic-update-slice_fusion), channel_id=1, source_target_pairs={{0,1},{1,0},{2,3},{3,2},{4,5},{5,4},{6,7},{7,6},{8,9},{9,8},{10,11... | collective-permute-start | bytes 798728 | tf_op jit(solution)/shard_map/ppermute | solution.py:233
  7.1 5.1 %copy-start.1 = (bf16[256,512]{1,0:T(8,128)(2,1)S(1)}, bf16[256,512]{1,0:T(8,128)(2,1)}, u32[]{:S(2)}) copy-start(bf16[256,512]{1,0:T(8,128)(2,1)} %param.8) | copy-start | bytes 786436
  8.0 20.7 %copy-start = (s32[16,16]{1,0:T(8,128)S(1)}, s32[16,16]{1,0:T(8,128)}, u32[]{:S(2)}) copy-start(s32[16,16]{1,0:T(8,128)} %mask_ref.3) | copy-start | bytes 3076
  8.0 20.7 %collective-permute-start.4 = (bf16[512,640]{1,0:T(8,128)(2,1)}, bf16[512,640]{1,0:T(8,128)(2,1)S(1)}, u32[]{:S(2)}, u32[]{:S(2)}) collective-permute-start(bf16[512,640]{1,0:T(8,128)(2,1)} %pad_maximum_fusion.1), channel_id=1, source_target_pairs={{0,1},{1,0},{2,3},{3,2},{4,5},{5,4},{6,7},{7,6},{8,9},{9,8},{10,11... | collective-permute-start | bytes 1966088 | tf_op jit(solution)/shard_map/ppermute | solution.py:233
  12.5 6.9 %collective-permute-start.3 = (bf16[1040,128]{1,0:T(8,128)(2,1)S(1)}, bf16[1040,128]{1,0:T(8,128)(2,1)S(1)}, u32[]{:S(2)}, u32[]{:S(2)}) collective-permute-start(bf16[1040,128]{1,0:T(8,128)(2,1)S(1)} %constant_dynamic-update-slice_fusion.1.kv0), channel_id=1, source_target_pairs={{0,4},{1,5},{2,6},{3,7},{4,0},{5,1},{6,2},{7,3},{8,12},{9,13},{10,... | collective-permute-start | bytes 798728 | tf_op jit(solution)/shard_map/ppermute | solution.py:233
  15.4 33.1 %collective-permute-start.6 = (bf16[512,640]{1,0:T(8,128)(2,1)}, bf16[512,640]{1,0:T(8,128)(2,1)S(1)}, u32[]{:S(2)}, u32[]{:S(2)}) collective-permute-start(bf16[512,640]{1,0:T(8,128)(2,1)} %pad_maximum_fusion.2), channel_id=1, source_target_pairs={{0,1},{1,0},{2,3},{3,2},{4,5},{5,4},{6,7},{7,6},{8,9},{9,8},{10,11... | collective-permute-start | bytes 1966088 | tf_op jit(solution)/shard_map/ppermute | solution.py:233
  15.6 11.0 %collective-permute-start.2 = (bf16[1040,128]{1,0:T(8,128)(2,1)S(1)}, bf16[1040,128]{1,0:T(8,128)(2,1)S(1)}, u32[]{:S(2)}, u32[]{:S(2)}) collective-permute-start(bf16[1040,128]{1,0:T(8,128)(2,1)S(1)} %constant_dynamic-update-slice_fusion.1.kv0), channel_id=1, source_target_pairs={{0,6},{1,7},{2,0},{3,1},{4,2},{5,3},{6,4},{7,5},{8,14},{9,15},{10,... | collective-permute-start | bytes 798728 | tf_op jit(solution)/shard_map/ppermute | solution.py:233
  16.7 9.9 %collective-permute-start.1 = (bf16[1040,128]{1,0:T(8,128)(2,1)S(1)}, bf16[1040,128]{1,0:T(8,128)(2,1)S(1)}, u32[]{:S(2)}, u32[]{:S(2)}) collective-permute-start(bf16[1040,128]{1,0:T(8,128)(2,1)S(1)} %constant_dynamic-update-slice_fusion.1.kv0), channel_id=1, source_target_pairs={{0,2},{1,3},{2,4},{3,5},{4,6},{5,7},{6,0},{7,1},{8,10},{9,11},{10,... | collective-permute-start | bytes 798728 | tf_op jit(solution)/shard_map/ppermute | solution.py:233
  19.4 26.7 %collective-permute-start.7 = (bf16[1040,128]{1,0:T(8,128)(2,1)S(1)}, bf16[1040,128]{1,0:T(8,128)(2,1)S(1)}, u32[]{:S(2)}, u32[]{:S(2)}) collective-permute-start(bf16[1040,128]{1,0:T(8,128)(2,1)S(1)} %get-tuple-element.31.kv0), channel_id=1, source_target_pairs={{0,2},{1,3},{2,4},{3,5},{4,6},{5,7},{6,0},{7,1},{8,10},{9,11},{10,... | collective-permute-start | bytes 798728 | tf_op jit(solution)/shard_map/ppermute | solution.py:233
  26.6 19.4 %collective-permute-start.8 = (bf16[1040,128]{1,0:T(8,128)(2,1)S(1)}, bf16[1040,128]{1,0:T(8,128)(2,1)S(1)}, u32[]{:S(2)}, u32[]{:S(2)}) collective-permute-start(bf16[1040,128]{1,0:T(8,128)(2,1)S(1)} %get-tuple-element.31.kv0), channel_id=1, source_target_pairs={{0,6},{1,7},{2,0},{3,1},{4,2},{5,3},{6,4},{7,5},{8,14},{9,15},{10,... | collective-permute-start | bytes 798728 | tf_op jit(solution)/shard_map/ppermute | solution.py:233
  26.6 21.9 %collective-permute-start.9 = (bf16[1040,128]{1,0:T(8,128)(2,1)S(1)}, bf16[1040,128]{1,0:T(8,128)(2,1)S(1)}, u32[]{:S(2)}, u32[]{:S(2)}) collective-permute-start(bf16[1040,128]{1,0:T(8,128)(2,1)S(1)} %get-tuple-element.31.kv0), channel_id=1, source_target_pairs={{0,4},{1,5},{2,6},{3,7},{4,0},{5,1},{6,2},{7,3},{8,12},{9,13},{10,... | collective-permute-start | bytes 798728 | tf_op jit(solution)/shard_map/ppermute | solution.py:233
  41.5 22.6 %collective-permute-start.11 = (bf16[1024,128]{1,0:T(8,128)(2,1)S(1)}, bf16[1024,128]{1,0:T(8,128)(2,1)S(1)}, u32[]{:S(2)}, u32[]{:S(2)}) collective-permute-start(bf16[1024,128]{1,0:T(8,128)(2,1)S(1)} %get-tuple-element.20), channel_id=1, source_target_pairs={{0,6},{1,7},{2,0},{3,1},{4,2},{5,3},{6,4},{7,5},{8,14},{9,15},{10,... | collective-permute-start | bytes 786440 | tf_op jit(solution)/shard_map/ppermute | solution.py:233
  46.0 21.8 %collective-permute-start.12 = (bf16[1024,128]{1,0:T(8,128)(2,1)S(1)}, bf16[1024,128]{1,0:T(8,128)(2,1)S(1)}, u32[]{:S(2)}, u32[]{:S(2)}) collective-permute-start(bf16[1024,128]{1,0:T(8,128)(2,1)S(1)} %get-tuple-element.21), channel_id=1, source_target_pairs={{0,2},{1,3},{2,4},{3,5},{4,6},{5,7},{6,0},{7,1},{8,10},{9,11},{10,... | collective-permute-start | bytes 786440 | tf_op jit(solution)/shard_map/ppermute | solution.py:233
  46.0 21.8 %collective-permute-start.13 = (bf16[1024,128]{1,0:T(8,128)(2,1)S(1)}, bf16[1024,128]{1,0:T(8,128)(2,1)S(1)}, u32[]{:S(2)}, u32[]{:S(2)}) collective-permute-start(bf16[1024,128]{1,0:T(8,128)(2,1)S(1)} %get-tuple-element.22), channel_id=1, source_target_pairs={{0,4},{1,5},{2,6},{3,7},{4,0},{5,1},{6,2},{7,3},{8,12},{9,13},{10,... | collective-permute-start | bytes 786440 | tf_op jit(solution)/shard_map/ppermute | solution.py:233
  61.2 8.2 %collective-permute-start.15 = (bf16[1024,128]{1,0:T(8,128)(2,1)S(1)}, bf16[1024,128]{1,0:T(8,128)(2,1)S(1)}, u32[]{:S(2)}, u32[]{:S(2)}) collective-permute-start(bf16[1024,128]{1,0:T(8,128)(2,1)S(1)} %get-tuple-element.24), channel_id=1, source_target_pairs={{0,6},{1,7},{2,0},{3,1},{4,2},{5,3},{6,4},{7,5},{8,14},{9,15},{10,... | collective-permute-start | bytes 786440 | tf_op jit(solution)/shard_map/ppermute | solution.py:233
  64.0 6.0 %collective-permute-start.16 = (bf16[1024,128]{1,0:T(8,128)(2,1)S(1)}, bf16[1024,128]{1,0:T(8,128)(2,1)S(1)}, u32[]{:S(2)}, u32[]{:S(2)}) collective-permute-start(bf16[1024,128]{1,0:T(8,128)(2,1)S(1)} %get-tuple-element.25), channel_id=1, source_target_pairs={{0,2},{1,3},{2,4},{3,5},{4,6},{5,7},{6,0},{7,1},{8,10},{9,11},{10,... | collective-permute-start | bytes 786440 | tf_op jit(solution)/shard_map/ppermute | solution.py:233
  64.0 7.7 %collective-permute-start.17 = (bf16[1024,128]{1,0:T(8,128)(2,1)S(1)}, bf16[1024,128]{1,0:T(8,128)(2,1)S(1)}, u32[]{:S(2)}, u32[]{:S(2)}) collective-permute-start(bf16[1024,128]{1,0:T(8,128)(2,1)S(1)} %get-tuple-element.26), channel_id=1, source_target_pairs={{0,4},{1,5},{2,6},{3,7},{4,0},{5,1},{6,2},{7,3},{8,12},{9,13},{10,... | collective-permute-start | bytes 786440 | tf_op jit(solution)/shard_map/ppermute | solution.py:233
  67.8 9.8 %collective-permute-start.5 = (bf16[256,640]{1,0:T(8,128)(2,1)S(1)}, bf16[256,640]{1,0:T(8,128)(2,1)S(1)}, u32[]{:S(2)}, u32[]{:S(2)}) collective-permute-start(bf16[256,640]{1,0:T(8,128)(2,1)S(1)} %get-tuple-element.16), channel_id=1, source_target_pairs={{0,1},{1,0},{2,3},{3,2},{4,5},{5,4},{6,7},{7,6},{8,9},{9,8},{10,11... | collective-permute-start | bytes 983048 | tf_op jit(solution)/shard_map/ppermute | solution.py:233
  67.8 14.3 %collective-permute-start.10 = (bf16[256,640]{1,0:T(8,128)(2,1)S(1)}, bf16[256,640]{1,0:T(8,128)(2,1)S(1)}, u32[]{:S(2)}, u32[]{:S(2)}) collective-permute-start(bf16[256,640]{1,0:T(8,128)(2,1)S(1)} %get-tuple-element.18), channel_id=1, source_target_pairs={{0,1},{1,0},{2,3},{3,2},{4,5},{5,4},{6,7},{7,6},{8,9},{9,8},{10,11... | collective-permute-start | bytes 983048 | tf_op jit(solution)/shard_map/ppermute | solution.py:233
  69.5 14.1 %collective-permute-start.14 = (bf16[512,128]{1,0:T(8,128)(2,1)S(1)}, bf16[512,128]{1,0:T(8,128)(2,1)S(1)}, u32[]{:S(2)}, u32[]{:S(2)}) collective-permute-start(bf16[512,128]{1,0:T(8,128)(2,1)S(1)} %pad_maximum_fusion.4), channel_id=1, source_target_pairs={{0,1},{1,0},{2,3},{3,2},{4,5},{5,4},{6,7},{7,6},{8,9},{9,8},{10,11... | collective-permute-start | bytes 393224 | tf_op jit(solution)/shard_map/ppermute | solution.py:233
  71.9 13.0 %collective-permute-start.18 = (bf16[512,128]{1,0:T(8,128)(2,1)S(1)}, bf16[512,128]{1,0:T(8,128)(2,1)S(1)}, u32[]{:S(2)}, u32[]{:S(2)}) collective-permute-start(bf16[512,128]{1,0:T(8,128)(2,1)S(1)} %pad_maximum_fusion.5), channel_id=1, source_target_pairs={{0,1},{1,0},{2,3},{3,2},{4,5},{5,4},{6,7},{7,6},{8,9},{9,8},{10,11... | collective-permute-start | bytes 393224 | tf_op jit(solution)/shard_map/ppermute | solution.py:233
